TPU v7x, 512 devices: a whole 4x4x16 slice. The times are simulated.
512 devices in a mesh: seq: 32 (over z, core), mp: 16 (over x, y).
Axes of the slice: x: 4, y: 4, z: 16, core: 2. Of those that a mesh axis runs over, the one named last changes fastest.
Arguments:
- qkv: bfloat16 [3, 65536, 4096], P(None, ('seq', 'mp')), may hold values from -6 to 6
- pack_segments: int32 [32, 64], replicated, may hold values from 0 to 63, as said below
- slot_offset: int32 [32], replicated, may hold values from 0 to 31, as said below
Outputs:
- attended: bfloat16 [65536, 4096], P('seq', 'mp')
Inputs may be any that keep to these rules, and one draw needn't show every extreme that they name: `pack_segments`: row p lists, for the 64 blocks of 32 tokens of pack p, the number of the image that each block belongs to: 0 for the first block, rising by one at each new image. An image has 1 or 2 blocks, and one of 2 blocks starts at an even block. `slot_offset`: each value once.
All inputs are finite; a program needn't handle non-finite values.
Results may differ from a plain program's by a relative error of at most 0.0047.
Values may be sent and summed in bfloat16 or wider, within the bound.
A program may use at most 64 MiB of HBM per device.

v0:
```python
import math

import jax
import jax.numpy as jnp
from jax import lax
from jax.sharding import PartitionSpec as P

HEAD = 128


def softmax_rows(scores):
    row_max = jnp.max(scores, axis=-1, keepdims=True)
    exponent = jnp.exp(scores - row_max)
    return (exponent / jnp.sum(exponent, axis=-1, keepdims=True)).astype(jnp.bfloat16)


def attend_rows(triple, segment):
    row_count = triple.shape[1]
    feature_width = triple.shape[2]
    head_count = feature_width // HEAD
    block_rows = math.gcd(row_count, 512)
    block_count = row_count // block_rows
    key_rows = triple[1].reshape(row_count, head_count, HEAD)
    value_rows = triple[2].reshape(row_count, head_count, HEAD)

    def one_block(block_index):
        first_row = block_index * block_rows
        queries = lax.dynamic_slice_in_dim(triple[0], first_row, block_rows, 0).reshape(
            block_rows, head_count, HEAD
        )
        query_segment = lax.dynamic_slice_in_dim(segment, first_row, block_rows, 0)
        scores = jnp.einsum(
            "qhd,khd->hqk", queries, key_rows, preferred_element_type=jnp.float32
        ) * HEAD ** (-0.5)
        same_image = query_segment[:, None] == segment[None, :]
        scores = jnp.where(same_image[None], scores, -jnp.inf)
        weights = softmax_rows(scores)
        result = jnp.einsum("hqk,khd->qhd", weights, value_rows, preferred_element_type=jnp.float32)
        return result.reshape(block_rows, feature_width).astype(jnp.bfloat16)

    blocks = lax.map(one_block, jnp.arange(block_count, dtype=jnp.int32))
    return blocks.reshape(row_count, feature_width)


def attend(triple, segment):
    return attend_rows(triple, segment)


def on_device(qkv, pack_segments, slot_offset):
    seq_count = lax.axis_size("seq")
    mp_count = lax.axis_size("mp")
    own_index = lax.axis_index("seq")
    local_rows = qkv.shape[1]
    loader_total = local_rows * mp_count
    pair = loader_total // seq_count
    half = pair // 2
    peers = jnp.arange(seq_count, dtype=jnp.int32)
    destinations = (own_index - slot_offset) % seq_count
    sources = (own_index + slot_offset) % seq_count
    send_order = jnp.sum(
        jnp.where(destinations[None, :] == peers[:, None], peers[None, :], 0), axis=1
    )
    loader_rows = lax.all_to_all(qkv, "mp", split_axis=2, concat_axis=1, tiled=True)
    width = loader_rows.shape[2]
    slots = loader_rows.reshape(3, seq_count, pair, width)
    outgoing = jnp.take(slots, send_order, axis=1)
    received = lax.all_to_all(outgoing, "seq", split_axis=1, concat_axis=1, tiled=True)
    packed = jnp.take(received, sources, axis=1).reshape(3, loader_total, width)
    pack_row = lax.dynamic_index_in_dim(pack_segments, own_index, 0, keepdims=False)
    segment = jnp.repeat(pack_row, half)
    return attend(packed, segment)


def solution(mesh):
    return jax.shard_map(
        on_device,
        mesh=mesh,
        in_specs=(P(None, ("seq", "mp"), None), P(), P()),
        out_specs=P("seq", "mp"),
        check_vma=False,
    )
```

profile of v0, /device:TPU:60, one launch (start us, length us, event | category | flops | bytes accessed | tf_op | source)
XLA Modules:
  0.0 329.7 jit_solution(6603841150666111084)
XLA Ops:
  0.0 7.2 %copy.30 = bf16[3,128,4096]{1,0,2:T(4,128)(2,1)} copy(bf16[3,128,4096]{2,1,0:T(8,128)(2,1)} %param.7) | data formatting | bytes 6291456 | tf_op args[0]
  7.2 7.2 %all-to-all-start = ((bf16[3,128,4096]{1,0,2:T(4,128)(2,1)}), bf16[3,128,4096]{1,0,2:T(4,128)(2,1)}, u32[]{:S(2)}, u32[]{:S(2)}) async-start(bf16[3,128,4096]{1,0,2:T(4,128)(2,1)} %copy.30), calls=%async_computation | async-start | bytes 8388608 | tf_op jit(solution)/shard_map/all_to_all | solution.py:63
  14.6 66.0 %all-to-all-done = bf16[3,128,4096]{1,0,2:T(4,128)(2,1)} async-done(((bf16[3,128,4096]{1,0,2:T(4,128)(2,1)}), bf16[3,128,4096]{1,0,2:T(4,128)(2,1)}, u32[]{:S(2)}, u32[]{:S(2)}) %all-to-all-start) | async-done | bytes 3145760 | tf_op jit(solution)/shard_map/all_to_all | solution.py:63
  80.7 2.6 copy.31
  83.3 2.8 copy.32
  86.2 2.6 gather_fusion
  88.8 2.0 select_bitcast_fusion.1
  90.8 15.4 %all-to-all-start.1 = ((bf16[3,32,64,256]{3,2,0,1:T(8,128)(2,1)}), bf16[3,32,64,256]{3,2,0,1:T(8,128)(2,1)S(1)}, u32[]{:S(2)}, u32[]{:S(2)}) async-start(bf16[3,32,64,256]{3,2,0,1:T(8,128)(2,1)} %select_bitcast_fusion.1), calls=%async_computation.1 | async-start | bytes 6291456 | tf_op jit(solution)/shard_map/all_to_all | solution.py:67
  106.4 145.0 %all-to-all-done.1 = bf16[3,32,64,256]{3,2,0,1:T(8,128)(2,1)S(1)} async-done(((bf16[3,32,64,256]{3,2,0,1:T(8,128)(2,1)}), bf16[3,32,64,256]{3,2,0,1:T(8,128)(2,1)S(1)}, u32[]{:S(2)}, u32[]{:S(2)}) %all-to-all-start.1) | async-done | bytes 3145760 | tf_op jit(solution)/shard_map/all_to_all | solution.py:67
  253.3 2.6 gather_fusion.1
  258.1 2.2 reshape_squeeze.6
  260.2 2.3 copy.36
  262.6 2.2 reshape_squeeze.7
  264.8 3.7 %copy.37 = bf16[2048,2,128]{0,2,1:T(8,128)(2,1)} copy(bf16[2048,2,128]{2,1,0:T(2,128)(2,1)} %reshape_squeeze.7) | data formatting | bytes 2097152
  268.5 3.2 copy.35
  271.6 58.0 %while.11 = (s32[]{:T(128)}, bf16[4,512,256]{2,1,0:T(8,128)(2,1)}, s32[4]{0:T(128)S(1)}, s32[2048]{0:T(1024)S(1)}, bf16[3,2048,256]{1,2,0:T(8,128)(2,1)}, /*inde...) while((s32[]{:T(128)}, bf16[4,512,256]{2,1,0:T(8,128)(2,1)}, ...), condition=%wide.region_4.6_spmd.clone, body=%wide.region_1.5_spmd.clone.sunk | while | flops 1087506432 | bytes 33602544 | solution.py:41
  275.1 5.2 %fusion.30 = (f32[2,512]{1,0:T(2,128)S(1)}, f32[2,512,2048]{2,1,0:T(8,128)}) fusion(pred[512,2048]{1,0:T(8,128)(4,1)S(1)} %broadcast_compare_fusion.2, bf16[512,2,128]{0,2,1:T(8,128)(2,1)S(1)} %bitcast.45, bf16[2048,2,128]{2,0,1:T(8,128)(2,1)S(1)} %copy-done.1), kind=kOutput, calls=%fused_computation.38.clone.1 | convolution fusion | flops 545261568 | bytes 10752000 | tf_op jit(solution)/shard_map/while/body/eval_jaxpr/sub | solution.py:13
  280.3 5.0 %fusion.31 = bf16[2,512,128]{1,2,0:T(8,128)(2,1)S(1)} fusion(bf16[2048,2,128]{0,2,1:T(8,128)(2,1)S(1)} %copy-done.2, f32[2,512,2048]{2,1,0:T(8,128)} %get-tuple-element.173, f32[2,512]{1,0:T(2,128)S(1)} %get-tuple-element.174), kind=kOutput, calls=%fused_computation.13.clone.1 | convolution fusion | flops 541196288 | bytes 9703424 | tf_op jit(solution)/shard_map/while/body/eval_jaxpr/hqk,khd->qhd/dot_general | solution.py:38
  289.6 5.2 %fusion.30 = (f32[2,512]{1,0:T(2,128)S(1)}, f32[2,512,2048]{2,1,0:T(8,128)}) fusion(pred[512,2048]{1,0:T(8,128)(4,1)S(1)} %broadcast_compare_fusion.2, bf16[512,2,128]{0,2,1:T(8,128)(2,1)S(1)} %bitcast.45, bf16[2048,2,128]{2,0,1:T(8,128)(2,1)S(1)} %copy-done.1), kind=kOutput, calls=%fused_computation.38.clone.1 | convolution fusion | flops 545261568 | bytes 10752000 | tf_op jit(solution)/shard_map/while/body/eval_jaxpr/sub | solution.py:13
  294.8 5.0 %fusion.31 = bf16[2,512,128]{1,2,0:T(8,128)(2,1)S(1)} fusion(bf16[2048,2,128]{0,2,1:T(8,128)(2,1)S(1)} %copy-done.2, f32[2,512,2048]{2,1,0:T(8,128)} %get-tuple-element.173, f32[2,512]{1,0:T(2,128)S(1)} %get-tuple-element.174), kind=kOutput, calls=%fused_computation.13.clone.1 | convolution fusion | flops 541196288 | bytes 9703424 | tf_op jit(solution)/shard_map/while/body/eval_jaxpr/hqk,khd->qhd/dot_general | solution.py:38
  304.1 5.2 %fusion.30 = (f32[2,512]{1,0:T(2,128)S(1)}, f32[2,512,2048]{2,1,0:T(8,128)}) fusion(pred[512,2048]{1,0:T(8,128)(4,1)S(1)} %broadcast_compare_fusion.2, bf16[512,2,128]{0,2,1:T(8,128)(2,1)S(1)} %bitcast.45, bf16[2048,2,128]{2,0,1:T(8,128)(2,1)S(1)} %copy-done.1), kind=kOutput, calls=%fused_computation.38.clone.1 | convolution fusion | flops 545261568 | bytes 10752000 | tf_op jit(solution)/shard_map/while/body/eval_jaxpr/sub | solution.py:13
  309.3 5.0 %fusion.31 = bf16[2,512,128]{1,2,0:T(8,128)(2,1)S(1)} fusion(bf16[2048,2,128]{0,2,1:T(8,128)(2,1)S(1)} %copy-done.2, f32[2,512,2048]{2,1,0:T(8,128)} %get-tuple-element.173, f32[2,512]{1,0:T(2,128)S(1)} %get-tuple-element.174), kind=kOutput, calls=%fused_computation.13.clone.1 | convolution fusion | flops 541196288 | bytes 9703424 | tf_op jit(solution)/shard_map/while/body/eval_jaxpr/hqk,khd->qhd/dot_general | solution.py:38
  318.6 5.2 %fusion.30 = (f32[2,512]{1,0:T(2,128)S(1)}, f32[2,512,2048]{2,1,0:T(8,128)}) fusion(pred[512,2048]{1,0:T(8,128)(4,1)S(1)} %broadcast_compare_fusion.2, bf16[512,2,128]{0,2,1:T(8,128)(2,1)S(1)} %bitcast.45, bf16[2048,2,128]{2,0,1:T(8,128)(2,1)S(1)} %copy-done.1), kind=kOutput, calls=%fused_computation.38.clone.1 | convolution fusion | flops 545261568 | bytes 10752000 | tf_op jit(solution)/shard_map/while/body/eval_jaxpr/sub | solution.py:13
  323.8 5.0 %fusion.31 = bf16[2,512,128]{1,2,0:T(8,128)(2,1)S(1)} fusion(bf16[2048,2,128]{0,2,1:T(8,128)(2,1)S(1)} %copy-done.2, f32[2,512,2048]{2,1,0:T(8,128)} %get-tuple-element.173, f32[2,512]{1,0:T(2,128)S(1)} %get-tuple-element.174), kind=kOutput, calls=%fused_computation.13.clone.1 | convolution fusion | flops 541196288 | bytes 9703424 | tf_op jit(solution)/shard_map/while/body/eval_jaxpr/hqk,khd->qhd/dot_general | solution.py:38
  (72 shorter events, 19.1 us)
Async XLA Ops:
  0.0 106.2 %copy-start = (s32[32,64]{1,0:T(8,128)S(1)}, s32[32,64]{1,0:T(8,128)}, u32[]{:S(2)}) copy-start(s32[32,64]{1,0:T(8,128)} %param.8) | copy-start | bytes 24580
  7.2 7.2 %copy-start.3 = (s32[32]{0:T(128)S(1)}, s32[32]{0:T(128)}, u32[]{:S(2)}) copy-start(s32[32]{0:T(128)} %param.9) | copy-start | bytes 388
  7.2 73.5 %all-to-all-start = ((bf16[3,128,4096]{1,0,2:T(4,128)(2,1)}), bf16[3,128,4096]{1,0,2:T(4,128)(2,1)}, u32[]{:S(2)}, u32[]{:S(2)}) async-start(bf16[3,128,4096]{1,0,2:T(4,128)(2,1)} %copy.30), calls=%async_computation | async-start | bytes 8388608 | tf_op jit(solution)/shard_map/all_to_all | solution.py:63
  90.8 160.6 %all-to-all-start.1 = ((bf16[3,32,64,256]{3,2,0,1:T(8,128)(2,1)}), bf16[3,32,64,256]{3,2,0,1:T(8,128)(2,1)S(1)}, u32[]{:S(2)}, u32[]{:S(2)}) async-start(bf16[3,32,64,256]{3,2,0,1:T(8,128)(2,1)} %select_bitcast_fusion.1), calls=%async_computation.1 | async-start | bytes 6291456 | tf_op jit(solution)/shard_map/all_to_all | solution.py:67
  271.6 3.5 %copy-start.1 = (bf16[2048,2,128]{2,0,1:T(8,128)(2,1)S(1)}, bf16[2048,2,128]{2,0,1:T(8,128)(2,1)}, u32[]{:S(2)}) copy-start(bf16[2048,2,128]{2,0,1:T(8,128)(2,1)} %get-tuple-element.204) | copy-start | bytes 3145732 | tf_op jit(solution)/shard_map/while
  275.1 5.2 %copy-start.2 = (bf16[2048,2,128]{0,2,1:T(8,128)(2,1)S(1)}, bf16[2048,2,128]{0,2,1:T(8,128)(2,1)}, u32[]{:S(2)}) copy-start(bf16[2048,2,128]{0,2,1:T(8,128)(2,1)} %get-tuple-element.205) | copy-start | bytes 3145732 | tf_op jit(solution)/shard_map/while
  286.2 3.5 %copy-start.1 = (bf16[2048,2,128]{2,0,1:T(8,128)(2,1)S(1)}, bf16[2048,2,128]{2,0,1:T(8,128)(2,1)}, u32[]{:S(2)}) copy-start(bf16[2048,2,128]{2,0,1:T(8,128)(2,1)} %get-tuple-element.204) | copy-start | bytes 3145732 | tf_op jit(solution)/shard_map/while
  289.6 5.2 %copy-start.2 = (bf16[2048,2,128]{0,2,1:T(8,128)(2,1)S(1)}, bf16[2048,2,128]{0,2,1:T(8,128)(2,1)}, u32[]{:S(2)}) copy-start(bf16[2048,2,128]{0,2,1:T(8,128)(2,1)} %get-tuple-element.205) | copy-start | bytes 3145732 | tf_op jit(solution)/shard_map/while
  300.7 3.5 %copy-start.1 = (bf16[2048,2,128]{2,0,1:T(8,128)(2,1)S(1)}, bf16[2048,2,128]{2,0,1:T(8,128)(2,1)}, u32[]{:S(2)}) copy-start(bf16[2048,2,128]{2,0,1:T(8,128)(2,1)} %get-tuple-element.204) | copy-start | bytes 3145732 | tf_op jit(solution)/shard_map/while
  304.1 5.2 %copy-start.2 = (bf16[2048,2,128]{0,2,1:T(8,128)(2,1)S(1)}, bf16[2048,2,128]{0,2,1:T(8,128)(2,1)}, u32[]{:S(2)}) copy-start(bf16[2048,2,128]{0,2,1:T(8,128)(2,1)} %get-tuple-element.205) | copy-start | bytes 3145732 | tf_op jit(solution)/shard_map/while
  315.2 3.5 %copy-start.1 = (bf16[2048,2,128]{2,0,1:T(8,128)(2,1)S(1)}, bf16[2048,2,128]{2,0,1:T(8,128)(2,1)}, u32[]{:S(2)}) copy-start(bf16[2048,2,128]{2,0,1:T(8,128)(2,1)} %get-tuple-element.204) | copy-start | bytes 3145732 | tf_op jit(solution)/shard_map/while
  318.6 5.2 %copy-start.2 = (bf16[2048,2,128]{0,2,1:T(8,128)(2,1)S(1)}, bf16[2048,2,128]{0,2,1:T(8,128)(2,1)}, u32[]{:S(2)}) copy-start(bf16[2048,2,128]{0,2,1:T(8,128)(2,1)} %get-tuple-element.205) | copy-start | bytes 3145732 | tf_op jit(solution)/shard_map/while
where the time goes:
time: 331 us; the launch traced here: 330 us
  waiting for transfers between devices  211 us (64%)
  local copies, waits for them, and re-layouts  47.5 us (14%)
  matrix products  40.6 us (12%)
  starting transfers between devices  22.6 us (7%)
  other arithmetic  5.19 us (2%)
    all_to_all x1, waiting for transfers between devices, on_device(): lax.all_to_all(outgoing, 'seq', split_axis=1, concat_axis=1, tiled=True)  145 us
    all_to_all x1, waiting for transfers between devices, on_device(): lax.all_to_all(qkv, 'mp', split_axis=2, concat_axis=1, tiled=True)  66 us
    sub x4, matrix products, softmax_rows(): exponent = jnp.exp(scores - row_max)  20.7 us
    dot_general x4, matrix products, one_block(): jnp.einsum('hqk,khd->qhd', weights, value_rows, preferred_element_type=jn...  19.9 us
    unnamed x8, local copies, waits for them, and re-layouts  16.4 us
    all_to_all x1, starting transfers between devices, on_device(): lax.all_to_all(outgoing, 'seq', split_axis=1, concat_axis=1, tiled=True)  15.4 us
    all_to_all x1, starting transfers between devices, on_device(): lax.all_to_all(qkv, 'mp', split_axis=2, concat_axis=1, tiled=True)  7.24 us
  transfers between devices with their start and end apart: 2, of which 2 were waited for; matrix products, arithmetic and copies ran while one was open for 0% of the time, Pallas kernels for 0%

commit v1 on v0

v1 whole, which is shorter than its diff:
```python
import functools
import math

import jax
import jax.numpy as jnp
from jax import lax
from jax.experimental import pallas as pl
from jax.experimental.pallas import tpu as pltpu
from jax.sharding import PartitionSpec as P

HEAD = 128
LOG2E = 1.4426950408889634
MESH = pl.DeviceIdType.MESH
SPLIT = 2
UNROLL = 4


def ring_peer(own, step, count):
    chips = count // 2
    k = step // 2
    away = chips // 2 - (k + 1) // 2
    turn = jnp.where(k % 2 == 1, away, chips - away)
    chip = (own // 2 + turn) % chips
    return 2 * chip + (own + step + 1) % 2


def kernel(
    seqs, mps, offset_ref, segment_ref, qkv_ref, out_ref,
    qkv_v, first_out, second_out, result, slot_v, slot_s,
    load_sem, slot_sem, first_send, first_recv, second_send, second_recv, out_sem, *landing,
):
    first_in, second_in = landing[:len(landing) // 2], landing[len(landing) // 2:]
    me = lax.axis_index("seq")
    group = lax.axis_index("mp")
    rows = qkv_ref.shape[1]
    slots = rows * mps // seqs
    own_slots = rows // slots
    heads = qkv_ref.shape[2] // HEAD
    mine = heads // mps
    part = slots // SPLIT

    def load(head):
        return pltpu.make_async_copy(
            qkv_ref.at[:, :, pl.ds(pl.multiple_of(head * HEAD, HEAD), HEAD)],
            qkv_v.at[head],
            load_sem.at[head],
        )

    def start_loads(step, carry):
        peer = (group + 1 + step % mps) % mps
        load(peer * mine + step // mps).start()
        return carry

    lax.fori_loop(0, heads, start_loads, 0)

    barrier = pltpu.get_barrier_semaphore()

    def greet_mp(step, carry):
        pl.semaphore_signal(
            barrier, inc=1, device_id=(me, (group + 1 + step) % mps), device_id_type=MESH
        )
        return carry

    def greet_seq(step, carry):
        pl.semaphore_signal(
            barrier, inc=1, device_id=((me + 1 + step) % seqs, group), device_id_type=MESH
        )
        return carry

    lax.fori_loop(0, mps - 1, greet_mp, 0)
    lax.fori_loop(0, seqs - 1, greet_seq, 0)

    lane = lax.broadcasted_iota(jnp.int32, (1, 128), 1)
    slot_of = jnp.zeros((1, 128), jnp.int32)
    for i in range(seqs):
        slot_of = jnp.where(lane == offset_ref[i], i, slot_of)
    slot_v[...] = slot_of
    slot_copy = pltpu.make_async_copy(slot_v, slot_s, slot_sem)
    slot_copy.start()

    row = lax.broadcasted_iota(jnp.int32, (rows, rows), 0)
    column = lax.broadcasted_iota(jnp.int32, (rows, rows), 1)
    meet = row // (slots // 2) == column // (slots // 2)
    for a in range(own_slots):
        slot = own_slots * group + a
        pack = (me - offset_ref[slot] + seqs) % seqs
        same = jnp.where(segment_ref[pack, 2 * slot] == segment_ref[pack, 2 * slot + 1], 1, 0)
        inside = (row // slots == a) & (column // slots == a)
        meet = meet | (inside & (jnp.full((rows, rows), same, jnp.int32) == 1))
    bias = jnp.where(meet, 0.0, -1e30)

    def attend(head):
        q, k, v = qkv_v[head, 0], qkv_v[head, 1], qkv_v[head, 2]
        scores = lax.dot_general(
            q, k, (((1,), (1,)), ((), ())), preferred_element_type=jnp.float32
        )
        scores = scores * (LOG2E / math.sqrt(HEAD)) + bias
        exponent = jnp.exp2(scores - jnp.max(scores, axis=-1, keepdims=True))
        weights = exponent / jnp.sum(exponent, axis=-1, keepdims=True)
        return jnp.dot(
            weights.astype(jnp.bfloat16), v, preferred_element_type=jnp.float32
        ).astype(jnp.bfloat16)

    def first_start(half, r, peer):
        c = half * SPLIT + r
        block = first_in[c].at[pl.ds(own_slots * group, own_slots)]

        @pl.when(peer != group)
        def _():
            pltpu.make_async_remote_copy(
                first_out.at[c, peer], block, first_send.at[c], first_recv.at[c],
                device_id=(me, peer), device_id_type=MESH,
            ).start()

        @pl.when(peer == group)
        def _():
            pltpu.make_async_copy(first_out.at[c, peer], block, first_recv.at[c]).start()

    def compute(half):
        def some_heads(step, carry):
            peers = [(group + 1 + step * UNROLL + u) % mps for u in range(UNROLL)]
            for peer in peers:
                load(peer * mine + half).wait()
            values = [attend(peer * mine + half) for peer in peers]
            for peer, value in zip(peers, values):
                value = value.reshape(own_slots, slots, HEAD)
                for r in range(SPLIT):
                    first_out[half * SPLIT + r, peer] = value[:, r * part:(r + 1) * part]
            for peer in peers:
                first_start(half, 0, peer)
            return carry

        def rest(r, step, carry):
            first_start(half, r, (group + 1 + step) % mps)
            return carry

        lax.fori_loop(0, mps // UNROLL, some_heads, 0)
        for r in range(1, SPLIT):
            lax.fori_loop(0, mps, functools.partial(rest, r), 0)

    def forward(c):
        pltpu.make_async_copy(first_in[c], first_in[c], first_recv.at[c]).wait()

        def send(step, carry):
            pack = ring_peer(me, step, seqs)
            slot = slot_s[0, (me - pack + seqs) % seqs]
            second_out[c, pack] = first_in[c][slot]
            pltpu.make_async_remote_copy(
                second_out.at[c, pack], second_in[c].at[me], second_send.at[c], second_recv.at[c],
                device_id=(pack, group), device_id_type=MESH,
            ).start()
            return carry

        lax.fori_loop(0, seqs - 1, send, 0)
        second_in[c][me] = first_in[c][slot_s[0, 0]]

    def finish(c):
        half, r = c // SPLIT, c % SPLIT
        landed = second_in[c].at[pl.ds(0, seqs - 1)]
        pltpu.make_async_copy(landed, landed, second_recv.at[c]).wait()

        def place(slot, carry):
            loader = (me + offset_ref[slot]) % seqs
            result[slot, r * part:(r + 1) * part, half * HEAD:(half + 1) * HEAD] = second_in[c][loader]
            return carry

        lax.fori_loop(0, seqs, place, 0)
        store(c).start()

    def store(c):
        half, r = c // SPLIT, c % SPLIT
        where = (slice(None), pl.ds(r * part, part), pl.ds(half * HEAD, HEAD))
        return pltpu.make_async_copy(result.at[where], out_ref.at[where], out_sem.at[c])

    chunks = mine * SPLIT
    pl.semaphore_wait(barrier, mps - 1 + seqs - 1)
    compute(0)
    slot_copy.wait()
    forward(0)
    for half in range(1, mine):
        compute(half)
    for c in range(1, chunks):
        forward(c)
        if c >= 2:
            finish(c - 2)
    for c in range(max(chunks - 2, 0), chunks):
        finish(c)
    for c in range(chunks):
        sent = first_out.at[c, pl.ds(0, mps - 1)]
        pltpu.make_async_copy(sent, sent, first_send.at[c]).wait()
        sent = second_out.at[c, pl.ds(0, seqs - 1)]
        pltpu.make_async_copy(sent, sent, second_send.at[c]).wait()
        store(c).wait()


def on_device(seqs, mps, qkv, pack_segments, slot_offset):
    members, rows, features = qkv.shape
    heads = features // HEAD
    mine = heads // mps
    slots = rows * mps // seqs
    own_slots = rows // slots
    part = slots // SPLIT
    chunks = mine * SPLIT
    smem = pl.BlockSpec(memory_space=pltpu.SMEM)
    out = pl.pallas_call(
        functools.partial(kernel, seqs, mps),
        out_shape=jax.ShapeDtypeStruct((seqs, slots, mine * HEAD), jnp.bfloat16),
        in_specs=[smem, smem, pl.BlockSpec(memory_space=pl.ANY)],
        out_specs=pl.BlockSpec(memory_space=pl.ANY),
        scratch_shapes=[
            pltpu.VMEM((heads, members, rows, HEAD), jnp.bfloat16),
            pltpu.VMEM((chunks, mps, own_slots, part, HEAD), jnp.bfloat16),
            pltpu.VMEM((chunks, seqs, part, HEAD), jnp.bfloat16),
            pltpu.VMEM((seqs, slots, mine * HEAD), jnp.bfloat16),
            pltpu.VMEM((1, 128), jnp.int32),
            pltpu.SMEM((1, 128), jnp.int32),
            pltpu.SemaphoreType.DMA((heads,)),
            pltpu.SemaphoreType.DMA,
            pltpu.SemaphoreType.DMA((chunks,)),
            pltpu.SemaphoreType.DMA((chunks,)),
            pltpu.SemaphoreType.DMA((chunks,)),
            pltpu.SemaphoreType.DMA((chunks,)),
            pltpu.SemaphoreType.DMA((chunks,)),
        ] + [pltpu.VMEM((seqs, part, HEAD), jnp.bfloat16)] * (2 * chunks),
        compiler_params=pltpu.CompilerParams(
            collective_id=0, has_side_effects=True, vmem_limit_bytes=32 * 1024 * 1024
        ),
        cost_estimate=pl.CostEstimate(
            flops=4 * heads * rows * rows * HEAD,
            bytes_accessed=2 * (members + 1) * rows * features,
            transcendentals=heads * rows * rows,
        ),
    )(slot_offset, pack_segments, qkv)
    return out.reshape(seqs * slots, mine * HEAD)


def solution(mesh):
    return jax.shard_map(
        functools.partial(on_device, mesh.shape["seq"], mesh.shape["mp"]),
        mesh=mesh,
        in_specs=(P(None, ("seq", "mp"), None), P(), P()),
        out_specs=P("seq", "mp"),
        check_vma=False,
    )
```

time: 331 us -> 82.8 us (0.25)
  the two profiles are of different devices: /device:TPU:60 before, /device:TPU:1 now
where the time goes in v1:
time: 82.8 us; the launch traced here: 81.5 us
  Pallas kernels  77.3 us (93%)
  local copies, waits for them, and re-layouts  4.23 us (5%)
    pallas_call x1, Pallas kernels, on_device(): pl.pallas_call(functools.partial(kernel, seqs, mps), out_shape=jax.ShapeD...  77.3 us
    unnamed x7, local copies, waits for them, and re-layouts  4.23 us

profile of v1, /device:TPU:1, one launch (start us, length us, event | category | flops | bytes accessed | tf_op | source)
XLA Modules:
  0.0 81.5 jit_solution(125418476387786434)
XLA Ops:
  0.0 0.0 copy-start
  0.0 1.9 %copy-done = bf16[3,128,4096]{2,1,0:T(8,128)(2,1)S(1)} copy-done((bf16[3,128,4096]{2,1,0:T(8,128)(2,1)S(1)}, bf16[3,128,4096]{2,1,0:T(8,128)(2,1)}, u32[]{:S(2)}) %copy-start) | copy-done | bytes 3145752
  1.9 0.0 copy-start.1
  1.9 0.7 copy-done.1
  2.6 0.0 copy-start.2
  2.6 0.7 copy-done.2
  3.3 77.3 %shard_map.37 = bf16[32,64,256]{2,1,0:T(8,128)(2,1)S(1)} custom-call(s32[32]{0:T(128)S(1)} %copy-done.2, s32[32,64]{1,0:T(8,128)S(1)} %copy-done.1, bf16[3,128,4096]{2,1,0:T(8,128)(2,1)S(1)} %copy-done), custom_call_target="tpu_custom_call" | custom-call | flops 268435456 | bytes 4194304 | tf_op jit(solution)/shard_map/pallas_call | solution.py:205
  80.5 1.0 %copy.5 = bf16[2048,256]{1,0:T(8,128)(2,1)} copy(bf16[2048,256]{1,0:T(8,128)(2,1)S(1)} %bitcast.1) | data formatting | bytes 2097152
Async XLA Ops:
  0.0 1.9 %copy-start = (bf16[3,128,4096]{2,1,0:T(8,128)(2,1)S(1)}, bf16[3,128,4096]{2,1,0:T(8,128)(2,1)}, u32[]{:S(2)}) copy-start(bf16[3,128,4096]{2,1,0:T(8,128)(2,1)} %qkv_ref.1) | copy-start | bytes 9437188
  1.9 0.7 copy-start.1
  2.6 0.7 copy-start.2

commit v2 on v1

v2 whole, which is shorter than its diff:
```python
import functools
import math

import jax
import jax.numpy as jnp
from jax import lax
from jax.experimental import pallas as pl
from jax.experimental.pallas import tpu as pltpu
from jax.sharding import PartitionSpec as P

HEAD = 128
LOG2E = 1.4426950408889634
MESH = pl.DeviceIdType.MESH
SPLIT = 2
UNROLL = 8


def ring_peer(own, step, count):
    chips = count // 2
    k = step // 2
    away = chips // 2 - (k + 1) // 2
    turn = jnp.where(k % 2 == 1, away, chips - away)
    chip = (own // 2 + turn) % chips
    return 2 * chip + (own + step + 1) % 2


def kernel(
    seqs, mps, offset_hbm, segment_hbm, qkv_ref, out_ref,
    qkv_v, first_out, second_out, offset_ref, segment_ref, slot_v, slot_s,
    load_sem, index_sem, first_send, first_recv, second_send, second_recv, word, *landing,
):
    first_in, second_in = landing[:len(landing) // 2], landing[len(landing) // 2:]
    me = lax.axis_index("seq")
    group = lax.axis_index("mp")
    rows = qkv_ref.shape[1]
    slots = rows * mps // seqs
    own_slots = rows // slots
    heads = qkv_ref.shape[2] // HEAD
    mine = heads // mps
    part = slots // SPLIT

    def load(head):
        return pltpu.make_async_copy(
            qkv_ref.at[:, :, pl.ds(pl.multiple_of(head * HEAD, HEAD), HEAD)],
            qkv_v.at[head],
            load_sem.at[head],
        )

    def start_loads(step, carry):
        peer = (group + 1 + step % mps) % mps
        load(peer * mine + step // mps).start()
        return carry

    offset_copy = pltpu.make_async_copy(offset_hbm, offset_ref, index_sem.at[0])
    segment_copy = pltpu.make_async_copy(segment_hbm, segment_ref, index_sem.at[1])
    offset_copy.start()
    segment_copy.start()
    lax.fori_loop(0, heads, start_loads, 0)

    core = me % 2
    barrier = pltpu.get_barrier_semaphore()
    sibling = (me + 1 - 2 * core, group)
    plane_others, ring_others = mps - 1, seqs // 2 - 1

    def greet_plane(step, carry):
        other = (me - core, (group + 1 + step) % mps)
        pl.semaphore_signal(barrier, inc=1, device_id=other, device_id_type=MESH)
        return carry

    def greet_ring(step, carry):
        other = ((me - core + 2 * (1 + step)) % seqs + 1, group)
        pl.semaphore_signal(barrier, inc=1, device_id=other, device_id_type=MESH)
        return carry

    pl.semaphore_signal(barrier, inc=1, device_id=sibling, device_id_type=MESH)
    lax.fori_loop(0, plane_others, greet_plane, 0)
    lax.fori_loop(0, ring_others, greet_ring, 0)

    def wait_plane():
        @pl.when(core == 0)
        def _():
            pl.semaphore_wait(barrier, 2 * plane_others + 1)
            pl.semaphore_signal(word, inc=1, device_id=sibling, device_id_type=MESH)

        @pl.when(core == 1)
        def _():
            pl.semaphore_wait(word, 1)

    def wait_ring():
        @pl.when(core == 0)
        def _():
            pl.semaphore_wait(word, 1)

        @pl.when(core == 1)
        def _():
            pl.semaphore_wait(barrier, 2 * ring_others + 1)
            pl.semaphore_signal(word, inc=1, device_id=sibling, device_id_type=MESH)

    offset_copy.wait()
    segment_copy.wait()

    lane = lax.broadcasted_iota(jnp.int32, (1, 128), 1)
    slot_of = jnp.zeros((1, 128), jnp.int32)
    for i in range(seqs):
        slot_of = jnp.where(lane == offset_ref[i], i, slot_of)
    slot_v[...] = slot_of
    slot_copy = pltpu.make_async_copy(slot_v, slot_s, index_sem.at[2])
    slot_copy.start()

    key = lax.broadcasted_iota(jnp.int32, (slots, rows), 0)
    query = lax.broadcasted_iota(jnp.int32, (slots, rows), 1)
    block = slots // 2
    meet = key // block == query % slots // block
    for a in range(own_slots):
        slot = own_slots * group + a
        pack = (me - offset_ref[slot] + seqs) % seqs
        same = jnp.where(segment_ref[pack, 2 * slot] == segment_ref[pack, 2 * slot + 1], 1, 0)
        meet = meet | ((query // slots == a) & (jnp.full((slots, rows), same, jnp.int32) == 1))
    bias = jnp.where(meet, 0.0, -1e30)
    own = [query // slots == a for a in range(own_slots)]
    diagonal = lax.broadcasted_iota(jnp.int32, (rows, rows), 0) == lax.broadcasted_iota(jnp.int32, (rows, rows), 1)
    identity = jnp.where(diagonal, 1.0, 0.0).astype(jnp.bfloat16)

    def attend(some):
        across = (((1,), (1,)), ((), ()))
        every = [
            lax.dot_general(qkv_v[h, 1], qkv_v[h, 0], across, preferred_element_type=jnp.float32) for h in some
        ]
        scores = []
        for x in every:
            mixed = x[:slots]
            for a in range(1, own_slots):
                mixed = jnp.where(own[a], x[a * slots:(a + 1) * slots], mixed)
            scores.append(mixed * (LOG2E / math.sqrt(HEAD)) + bias)
        peaks = [jnp.max(x, axis=0, keepdims=True) for x in scores]
        exponents = [jnp.exp2(x - peak) for x, peak in zip(scores, peaks)]
        totals = [1.0 / jnp.sum(x, axis=0, keepdims=True) for x in exponents]
        weights = [x * total for x, total in zip(exponents, totals)]
        weights = [
            jnp.concatenate([jnp.where(mask, x, 0.0) for mask in own], axis=0).astype(jnp.bfloat16) for x in weights
        ]
        turned = [
            lax.dot_general(identity, x, across, preferred_element_type=jnp.float32).astype(jnp.bfloat16)
            for x in weights
        ]
        return [
            jnp.dot(x, qkv_v[h, 2], preferred_element_type=jnp.float32).astype(jnp.bfloat16)
            for x, h in zip(turned, some)
        ]

    def first_start(c, peer):
        block = first_in[c].at[pl.ds(own_slots * group, own_slots)]

        @pl.when(peer != group)
        def _():
            pltpu.make_async_remote_copy(
                first_out.at[c, peer], block, first_send.at[c], first_recv.at[c],
                device_id=(me, peer), device_id_type=MESH,
            ).start()

        @pl.when(peer == group)
        def _():
            pltpu.make_async_copy(first_out.at[c, peer], block, first_recv.at[c]).start()

    def compute(half):
        def some_heads(step, carry):
            peers = [(group + 1 + step * UNROLL + u) % mps for u in range(UNROLL)]
            for peer in peers:
                load(peer * mine + half).wait()
            values = attend([peer * mine + half for peer in peers])
            for peer, value in zip(peers, values):
                value = value.reshape(own_slots, slots, HEAD)
                for r in range(SPLIT):
                    first_out[half * SPLIT + r, peer] = value[:, r * part:(r + 1) * part]
            return carry

        lax.fori_loop(0, mps // UNROLL, some_heads, 0)

    def spread(c):
        def one(step, carry):
            first_start(c, (group + 1 + step) % mps)
            return carry

        lax.fori_loop(0, mps, one, 0)

    def forward(c):
        def send(step, carry):
            pack = ring_peer(me, step, seqs)
            slot = slot_s[0, (me - pack + seqs) % seqs]
            second_out[c, pack] = first_in[c][slot]
            pltpu.make_async_remote_copy(
                second_out.at[c, pack], second_in[c].at[me], second_send.at[c], second_recv.at[c],
                device_id=(pack, group), device_id_type=MESH,
            ).start()
            return carry

        lax.fori_loop(0, seqs - 1, send, 0)
        second_in[c][me] = first_in[c][slot_s[0, 0]]

    def finish(c):
        half, r = c // SPLIT, c % SPLIT
        landed = second_in[c].at[pl.ds(0, seqs - 1)]
        pltpu.make_async_copy(landed, landed, second_recv.at[c]).wait()

        def place(slot, carry):
            loader = (me + offset_ref[slot]) % seqs
            out_ref[slot, r * part:(r + 1) * part, half * HEAD:(half + 1) * HEAD] = second_in[c][loader]
            return carry

        lax.fori_loop(0, seqs, place, 0)

    chunks = mine * SPLIT
    compute(0)
    wait_plane()
    for c in range(SPLIT):
        spread(c)
    slot_copy.wait()
    for c in range(chunks):
        pltpu.make_async_copy(first_in[c], first_in[c], first_recv.at[c]).wait()
        if c == 0:
            wait_ring()
        forward(c)
        if (c + 1) % SPLIT == 0 and c + 1 < chunks:
            compute((c + 1) // SPLIT)
            for other in range(c + 1, c + 1 + SPLIT):
                spread(other)
    for c in range(chunks):
        finish(c)
    for c in range(chunks):
        sent = first_out.at[c, pl.ds(0, mps - 1)]
        pltpu.make_async_copy(sent, sent, first_send.at[c]).wait()
        sent = second_out.at[c, pl.ds(0, seqs - 1)]
        pltpu.make_async_copy(sent, sent, second_send.at[c]).wait()


def on_device(seqs, mps, qkv, pack_segments, slot_offset):
    members, rows, features = qkv.shape
    heads = features // HEAD
    mine = heads // mps
    slots = rows * mps // seqs
    own_slots = rows // slots
    part = slots // SPLIT
    chunks = mine * SPLIT
    hbm = pl.BlockSpec(memory_space=pltpu.HBM)
    out = pl.pallas_call(
        functools.partial(kernel, seqs, mps),
        out_shape=jax.ShapeDtypeStruct((seqs, slots, mine * HEAD), jnp.bfloat16),
        in_specs=[hbm, hbm, hbm],
        out_specs=pl.BlockSpec(memory_space=pltpu.VMEM),
        scratch_shapes=[
            pltpu.VMEM((heads, members, rows, HEAD), jnp.bfloat16),
            pltpu.VMEM((chunks, mps, own_slots, part, HEAD), jnp.bfloat16),
            pltpu.VMEM((chunks, seqs, part, HEAD), jnp.bfloat16),
            pltpu.SMEM(slot_offset.shape, jnp.int32),
            pltpu.SMEM(pack_segments.shape, jnp.int32),
            pltpu.VMEM((1, 128), jnp.int32),
            pltpu.SMEM((1, 128), jnp.int32),
            pltpu.SemaphoreType.DMA((heads,)),
            pltpu.SemaphoreType.DMA((3,)),
            pltpu.SemaphoreType.DMA((chunks,)),
            pltpu.SemaphoreType.DMA((chunks,)),
            pltpu.SemaphoreType.DMA((chunks,)),
            pltpu.SemaphoreType.DMA((chunks,)),
            pltpu.SemaphoreType.REGULAR,
        ] + [pltpu.VMEM((seqs, part, HEAD), jnp.bfloat16)] * (2 * chunks),
        compiler_params=pltpu.CompilerParams(
            collective_id=0, has_side_effects=True, vmem_limit_bytes=32 * 1024 * 1024
        ),
        cost_estimate=pl.CostEstimate(
            flops=4 * heads * rows * rows * HEAD,
            bytes_accessed=2 * (members + 1) * rows * features,
            transcendentals=heads * rows * rows,
        ),
    )(*(pltpu.with_memory_space_constraint(x, pltpu.HBM) for x in (slot_offset, pack_segments, qkv)))
    return out.reshape(seqs * slots, mine * HEAD)


def solution(mesh):
    return jax.shard_map(
        functools.partial(on_device, mesh.shape["seq"], mesh.shape["mp"]),
        mesh=mesh,
        in_specs=(P(None, ("seq", "mp"), None), P(), P()),
        out_specs=P("seq", "mp"),
        check_vma=False,
    )
```

time: 82.8 us -> 70.6 us (0.85); the launches traced: 81.5 us -> 70.4 us
  Pallas kernels: 77.3 us -> 69.4 us
  local copies, waits for them, and re-layouts: 4.23 us -> 0.97 us
    pallas_call x1, Pallas kernels: 77.3 us -> 69.4 us  [on_device(): pl.pallas_call(functools.partial(kernel, seqs, mps), out_shape=jax.ShapeD...]
    unnamed x7 -> x1, local copies, waits for them, and re-layouts: 4.23 us -> 0.97 us
where the time goes in v2:
time: 70.6 us; the launch traced here: 70.4 us
  Pallas kernels  69.4 us (98%)
  local copies, waits for them, and re-layouts  0.97 us (1%)
    pallas_call x1, Pallas kernels, on_device(): pl.pallas_call(functools.partial(kernel, seqs, mps), out_shape=jax.ShapeD...  69.4 us

profile of v2, /device:TPU:1, one launch (start us, length us, event | category | flops | bytes accessed | tf_op | source)
XLA Modules:
  0.0 70.4 jit_solution(15439565329081705428)
XLA Ops:
  0.0 69.4 %shard_map.37 = bf16[32,64,256]{2,1,0:T(8,128)(2,1)S(1)} custom-call(s32[32]{0:T(128)} %offset_hbm.1, s32[32,64]{1,0:T(8,128)} %segment_hbm.1, bf16[3,128,4096]{2,1,0:T(8,128)(2,1)} %qkv_ref.1), custom_call_target="tpu_custom_call" | custom-call | flops 268435456 | bytes 4194304 | tf_op jit(solution)/shard_map/pallas_call | solution.py:245
  69.4 1.0 %copy.5 = bf16[2048,256]{1,0:T(8,128)(2,1)} copy(bf16[2048,256]{1,0:T(8,128)(2,1)S(1)} %bitcast.1) | data formatting | bytes 2097152

commit v3 on v2

--- a/solution.py
+++ b/solution.py
@@ -9,9 +9,10 @@
 from jax.sharding import PartitionSpec as P
 
 HEAD = 128
+AHEAD = 2
 LOG2E = 1.4426950408889634
 MESH = pl.DeviceIdType.MESH
-SPLIT = 2
+CHUNKS = ((0, 0, 16), (0, 16, 32), (0, 32, 64), (1, 0, 64))
 UNROLL = 8
 
 
@@ -26,10 +27,11 @@
 
 def kernel(
     seqs, mps, offset_hbm, segment_hbm, qkv_ref, out_ref,
-    qkv_v, first_out, second_out, offset_ref, segment_ref, slot_v, slot_s,
+    qkv_v, offset_ref, segment_ref, slot_v, slot_s,
     load_sem, index_sem, first_send, first_recv, second_send, second_recv, word, *landing,
 ):
-    first_in, second_in = landing[:len(landing) // 2], landing[len(landing) // 2:]
+    chunks = len(CHUNKS)
+    first_out, first_in, second_out, second_in = (landing[i * chunks:(i + 1) * chunks] for i in range(4))
     me = lax.axis_index("seq")
     group = lax.axis_index("mp")
     rows = qkv_ref.shape[1]
@@ -37,7 +39,6 @@
     own_slots = rows // slots
     heads = qkv_ref.shape[2] // HEAD
     mine = heads // mps
-    part = slots // SPLIT
 
     def load(head):
         return pltpu.make_async_copy(
@@ -154,13 +155,13 @@
         @pl.when(peer != group)
         def _():
             pltpu.make_async_remote_copy(
-                first_out.at[c, peer], block, first_send.at[c], first_recv.at[c],
+                first_out[c].at[peer], block, first_send.at[c], first_recv.at[c],
                 device_id=(me, peer), device_id_type=MESH,
             ).start()
 
         @pl.when(peer == group)
         def _():
-            pltpu.make_async_copy(first_out.at[c, peer], block, first_recv.at[c]).start()
+            pltpu.make_async_copy(first_out[c].at[peer], block, first_recv.at[c]).start()
 
     def compute(half):
         def some_heads(step, carry):
@@ -170,8 +171,9 @@
             values = attend([peer * mine + half for peer in peers])
             for peer, value in zip(peers, values):
                 value = value.reshape(own_slots, slots, HEAD)
-                for r in range(SPLIT):
-                    first_out[half * SPLIT + r, peer] = value[:, r * part:(r + 1) * part]
+                for c, (head, start, stop) in enumerate(CHUNKS):
+                    if head == half:
+                        first_out[c][peer] = value[:, start:stop]
             return carry
 
         lax.fori_loop(0, mps // UNROLL, some_heads, 0)
@@ -181,55 +183,56 @@
             first_start(c, (group + 1 + step) % mps)
             return carry
 
-        lax.fori_loop(0, mps, one, 0)
+        lax.fori_loop(0, mps, one, 0, unroll=4)
 
     def forward(c):
         def send(step, carry):
             pack = ring_peer(me, step, seqs)
             slot = slot_s[0, (me - pack + seqs) % seqs]
-            second_out[c, pack] = first_in[c][slot]
+            second_out[c][pack] = first_in[c][slot]
             pltpu.make_async_remote_copy(
-                second_out.at[c, pack], second_in[c].at[me], second_send.at[c], second_recv.at[c],
+                second_out[c].at[pack], second_in[c].at[me], second_send.at[c], second_recv.at[c],
                 device_id=(pack, group), device_id_type=MESH,
             ).start()
             return carry
 
-        lax.fori_loop(0, seqs - 1, send, 0)
+        lax.fori_loop(0, seqs - 1, send, 0, unroll=31)
         second_in[c][me] = first_in[c][slot_s[0, 0]]
 
     def finish(c):
-        half, r = c // SPLIT, c % SPLIT
+        half, start, stop = CHUNKS[c]
         landed = second_in[c].at[pl.ds(0, seqs - 1)]
         pltpu.make_async_copy(landed, landed, second_recv.at[c]).wait()
 
         def place(slot, carry):
             loader = (me + offset_ref[slot]) % seqs
-            out_ref[slot, r * part:(r + 1) * part, half * HEAD:(half + 1) * HEAD] = second_in[c][loader]
-            return carry
-
-        lax.fori_loop(0, seqs, place, 0)
-
-    chunks = mine * SPLIT
+            out_ref[slot, start:stop, half * HEAD:(half + 1) * HEAD] = second_in[c][loader]
+            return carry
+
+        lax.fori_loop(0, seqs, place, 0, unroll=8)
+
     compute(0)
     wait_plane()
-    for c in range(SPLIT):
+    for c in range(AHEAD):
         spread(c)
     slot_copy.wait()
+    wait_ring()
     for c in range(chunks):
+        if CHUNKS[c][0] > 0 and CHUNKS[c][1] == 0:
+            compute(CHUNKS[c][0])
+            for other in range(c, chunks):
+                if CHUNKS[other][0] == CHUNKS[c][0]:
+                    spread(other)
         pltpu.make_async_copy(first_in[c], first_in[c], first_recv.at[c]).wait()
-        if c == 0:
-            wait_ring()
+        if c + AHEAD < chunks and CHUNKS[c + AHEAD][0] == 0:
+            spread(c + AHEAD)
         forward(c)
-        if (c + 1) % SPLIT == 0 and c + 1 < chunks:
-            compute((c + 1) // SPLIT)
-            for other in range(c + 1, c + 1 + SPLIT):
-                spread(other)
     for c in range(chunks):
         finish(c)
     for c in range(chunks):
-        sent = first_out.at[c, pl.ds(0, mps - 1)]
+        sent = first_out[c].at[pl.ds(0, mps - 1)]
         pltpu.make_async_copy(sent, sent, first_send.at[c]).wait()
-        sent = second_out.at[c, pl.ds(0, seqs - 1)]
+        sent = second_out[c].at[pl.ds(0, seqs - 1)]
         pltpu.make_async_copy(sent, sent, second_send.at[c]).wait()
 
 
@@ -239,8 +242,10 @@
     mine = heads // mps
     slots = rows * mps // seqs
     own_slots = rows // slots
-    part = slots // SPLIT
-    chunks = mine * SPLIT
+    chunks = len(CHUNKS)
+    parts = [stop - start for _, start, stop in CHUNKS]
+    by_loader = [pltpu.VMEM((seqs, part, HEAD), jnp.bfloat16) for part in parts]
+    by_group = [pltpu.VMEM((mps, own_slots, part, HEAD), jnp.bfloat16) for part in parts]
     hbm = pl.BlockSpec(memory_space=pltpu.HBM)
     out = pl.pallas_call(
         functools.partial(kernel, seqs, mps),
@@ -249,8 +254,6 @@
         out_specs=pl.BlockSpec(memory_space=pltpu.VMEM),
         scratch_shapes=[
             pltpu.VMEM((heads, members, rows, HEAD), jnp.bfloat16),
-            pltpu.VMEM((chunks, mps, own_slots, part, HEAD), jnp.bfloat16),
-            pltpu.VMEM((chunks, seqs, part, HEAD), jnp.bfloat16),
             pltpu.SMEM(slot_offset.shape, jnp.int32),
             pltpu.SMEM(pack_segments.shape, jnp.int32),
             pltpu.VMEM((1, 128), jnp.int32),
@@ -262,7 +265,7 @@
             pltpu.SemaphoreType.DMA((chunks,)),
             pltpu.SemaphoreType.DMA((chunks,)),
             pltpu.SemaphoreType.REGULAR,
-        ] + [pltpu.VMEM((seqs, part, HEAD), jnp.bfloat16)] * (2 * chunks),
+        ] + by_group + 3 * by_loader,
         compiler_params=pltpu.CompilerParams(
             collective_id=0, has_side_effects=True, vmem_limit_bytes=32 * 1024 * 1024
         ),

time: 70.6 us -> 68.7 us (0.973)
  Pallas kernels: 69.4 us -> 67.6 us
    pallas_call x1, Pallas kernels: 69.4 us -> 67.6 us  [on_device(): pl.pallas_call(functools.partial(kernel, seqs, mps), out_shape=jax.ShapeD...]
where the time goes in v3:
time: 68.7 us; the launch traced here: 68.6 us
  Pallas kernels  67.6 us (98%)
  local copies, waits for them, and re-layouts  0.97 us (1%)
    pallas_call x1, Pallas kernels, on_device(): pl.pallas_call(functools.partial(kernel, seqs, mps), out_shape=jax.ShapeD...  67.6 us

profile of v3, /device:TPU:1, one launch (start us, length us, event | category | flops | bytes accessed | tf_op | source)
XLA Modules:
  0.0 68.6 jit_solution(176013481978538016)
XLA Ops:
  0.0 67.6 %shard_map.37 = bf16[32,64,256]{2,1,0:T(8,128)(2,1)S(1)} custom-call(s32[32]{0:T(128)} %offset_hbm.1, s32[32,64]{1,0:T(8,128)} %segment_hbm.1, bf16[3,128,4096]{2,1,0:T(8,128)(2,1)} %qkv_ref.1), custom_call_target="tpu_custom_call" | custom-call | flops 268435456 | bytes 4194304 | tf_op jit(solution)/shard_map/pallas_call | solution.py:250
  67.6 1.0 %copy.5 = bf16[2048,256]{1,0:T(8,128)(2,1)} copy(bf16[2048,256]{1,0:T(8,128)(2,1)S(1)} %bitcast.1) | data formatting | bytes 2097152

commit v4 on v3

--- a/solution.py
+++ b/solution.py
@@ -56,7 +56,6 @@
     segment_copy = pltpu.make_async_copy(segment_hbm, segment_ref, index_sem.at[1])
     offset_copy.start()
     segment_copy.start()
-    lax.fori_loop(0, heads, start_loads, 0)
 
     core = me % 2
     barrier = pltpu.get_barrier_semaphore()
@@ -74,8 +73,10 @@
         return carry
 
     pl.semaphore_signal(barrier, inc=1, device_id=sibling, device_id_type=MESH)
-    lax.fori_loop(0, plane_others, greet_plane, 0)
-    lax.fori_loop(0, ring_others, greet_ring, 0)
+    lax.fori_loop(0, plane_others, greet_plane, 0, unroll=5)
+    lax.fori_loop(0, mps, start_loads, 0, unroll=4)
+    lax.fori_loop(0, ring_others, greet_ring, 0, unroll=5)
+    lax.fori_loop(mps, heads, start_loads, 0, unroll=4)
 
     def wait_plane():
         @pl.when(core == 0)

time: 68.7 us -> 68.8 us (level)
  no operation moved by 1% of the time
where the time goes in v4:
time: 68.8 us; the launch traced here: 68.7 us
  Pallas kernels  67.7 us (98%)
  local copies, waits for them, and re-layouts  0.97 us (1%)
    pallas_call x1, Pallas kernels, on_device(): pl.pallas_call(functools.partial(kernel, seqs, mps), out_shape=jax.ShapeD...  67.7 us

profile of v4, /device:TPU:1, one launch (start us, length us, event | category | flops | bytes accessed | tf_op | source)
XLA Modules:
  0.0 68.7 jit_solution(15105245070957341661)
XLA Ops:
  0.0 67.7 %shard_map.37 = bf16[32,64,256]{2,1,0:T(8,128)(2,1)S(1)} custom-call(s32[32]{0:T(128)} %offset_hbm.1, s32[32,64]{1,0:T(8,128)} %segment_hbm.1, bf16[3,128,4096]{2,1,0:T(8,128)(2,1)} %qkv_ref.1), custom_call_target="tpu_custom_call" | custom-call | flops 268435456 | bytes 4194304 | tf_op jit(solution)/shard_map/pallas_call | solution.py:251
  67.7 1.0 %copy.5 = bf16[2048,256]{1,0:T(8,128)(2,1)} copy(bf16[2048,256]{1,0:T(8,128)(2,1)S(1)} %bitcast.1) | data formatting | bytes 2097152

commit v5 on v3

--- a/solution.py
+++ b/solution.py
@@ -23,6 +23,12 @@
     turn = jnp.where(k % 2 == 1, away, chips - away)
     chip = (own // 2 + turn) % chips
     return 2 * chip + (own + step + 1) % 2
+
+
+def plane_order(count):
+    side = math.isqrt(count)
+    steps = [(across, down) for across in range(side) for down in range(side)]
+    return sorted(steps, key=lambda step: -sum(min(way, side - way) for way in step))
 
 
 def kernel(
@@ -179,11 +185,9 @@
         lax.fori_loop(0, mps // UNROLL, some_heads, 0)
 
     def spread(c):
-        def one(step, carry):
-            first_start(c, (group + 1 + step) % mps)
-            return carry
-
-        lax.fori_loop(0, mps, one, 0, unroll=4)
+        for across, down in plane_order(mps):
+            side = math.isqrt(mps)
+            first_start(c, (group // side + across) % side * side + (group + down) % side)
 
     def forward(c):
         def send(step, carry):

time: 68.7 us -> 68.6 us (level)
  no operation moved by 1% of the time
where the time goes in v5:
time: 68.6 us; the launch traced here: 68.4 us
  Pallas kernels  67.5 us (98%)
  local copies, waits for them, and re-layouts  0.97 us (1%)
    pallas_call x1, Pallas kernels, on_device(): pl.pallas_call(functools.partial(kernel, seqs, mps), out_shape=jax.ShapeD...  67.5 us

profile of v5, /device:TPU:1, one launch (start us, length us, event | category | flops | bytes accessed | tf_op | source)
XLA Modules:
  0.0 68.4 jit_solution(17362427747961303948)
XLA Ops:
  0.0 67.5 %shard_map.37 = bf16[32,64,256]{2,1,0:T(8,128)(2,1)S(1)} custom-call(s32[32]{0:T(128)} %offset_hbm.1, s32[32,64]{1,0:T(8,128)} %segment_hbm.1, bf16[3,128,4096]{2,1,0:T(8,128)(2,1)} %qkv_ref.1), custom_call_target="tpu_custom_call" | custom-call | flops 268435456 | bytes 4194304 | tf_op jit(solution)/shard_map/pallas_call | solution.py:254
  67.5 1.0 %copy.5 = bf16[2048,256]{1,0:T(8,128)(2,1)} copy(bf16[2048,256]{1,0:T(8,128)(2,1)S(1)} %bitcast.1) | data formatting | bytes 2097152
